TPU v7x, 32 devices: a whole 2x2x4 slice. The times are simulated.
32 devices in a mesh: dp: 4 (over y, core), expert: 8 (over z, x).
Axes of the slice: x: 2, y: 2, z: 4, core: 2. Of those that a mesh axis runs over, the one named last changes fastest.
Arguments:
- tokens: bfloat16 [4096, 1024], P(('dp', 'expert')), may hold values from -6 to 6
- expert_ids: int32 [4096, 8], P(('dp', 'expert')), may hold values from 0 to 31, as said below
- route_num: int32 [4096, 8], P(('dp', 'expert')), may hold values from 1 to 256
- w_gate: bfloat16 [32, 1024, 384], P('expert'), may hold values from -0.1875 to 0.1875
- w_up: bfloat16 [32, 1024, 384], P('expert'), may hold values from -0.1875 to 0.1875
- w_down: bfloat16 [32, 384, 1024], P('expert'), may hold values from -0.3125 to 0.3125
- cotangent: bfloat16 [4096, 1024], P(('dp', 'expert')), may hold values from -1.1953125 to 1.1953125
Outputs:
- output: bfloat16 [4096, 1024], P(('dp', 'expert'))
- tokens_grad: bfloat16 [4096, 1024], P(('dp', 'expert'))
- w_gate_grad: bfloat16 [32, 1024, 384], P('expert', 'dp')
- w_up_grad: bfloat16 [32, 1024, 384], P('expert', 'dp')
- w_down_grad: bfloat16 [32, 384, 1024], P('expert', None, 'dp')
Inputs may be any that keep to these rules, and one draw needn't show every extreme that they name: `expert_ids`: each row names 8 different experts. Rows come in aligned blocks of 128, one device's tokens each, and 8 consecutive blocks form one data group. In each data group one expert is named by exactly 40 rows of every block of that group, and in no block is any expert named by more than 40 rows.
All inputs are finite; a program needn't handle non-finite values.
Results may differ from a plain program's by a relative error of at most 0.017.
Values may be sent and summed in bfloat16 or wider, within the bound.
A program may use at most 128 MiB of HBM per device.

v0:
```python
import jax
import jax.numpy as jnp
from jax import lax
from jax.sharding import PartitionSpec as P

DENOM = 256


def local(tokens, expert_ids, route_num, w_gate, w_up, w_down, cotangent):
    exp_dev = w_gate.shape[0]
    width = tokens.shape[1]
    ranks = lax.axis_size("expert")
    rows = tokens.shape[0]
    capacity = 5 * rows // 16
    bf16, f32 = jnp.bfloat16, jnp.float32

    packed = lax.all_gather(expert_ids * 512 + route_num, "expert")
    x_all = lax.all_gather(tokens, "expert")
    c_all = lax.all_gather(cotangent, "expert")

    ids, num = packed // 512, packed % 512
    first = lax.axis_index("expert") * exp_dev
    mine = first + jnp.arange(exp_dev, dtype=jnp.int32)
    named = ids[:, :, :, None] == mine
    match = jnp.any(named, axis=2)
    weight = jnp.sum(jnp.where(named, num[..., None], 0), axis=2).astype(f32) / DENOM
    earlier = jnp.tril(jnp.ones((rows, rows), bf16), -1)
    rank = jnp.einsum("ut,bte->beu", earlier, match.astype(bf16), preferred_element_type=f32)
    slot = jnp.where(match.transpose(0, 2, 1), rank.astype(jnp.int32), -1)
    place = slot[:, :, None, :] == jnp.arange(capacity, dtype=jnp.int32)[:, None]
    pick = place.astype(bf16)
    pick_w = jnp.where(place, weight.transpose(0, 2, 1)[:, :, None, :], 0.0).astype(bf16)
    pick = pick.reshape(ranks, exp_dev * capacity, rows)
    pick_w = pick_w.reshape(ranks, exp_dev * capacity, rows)

    def to_slots(sel, vals):
        got = jnp.einsum("bst,btd->bsd", sel, vals, preferred_element_type=f32).astype(bf16)
        got = got.reshape(ranks, exp_dev, capacity, width).transpose(1, 0, 2, 3)
        return got.reshape(exp_dev, ranks * capacity, width)

    def from_slots(sel, vals):
        vals = vals.reshape(exp_dev, ranks, capacity, width).transpose(1, 0, 2, 3)
        vals = vals.reshape(ranks, exp_dev * capacity, width)
        part = jnp.einsum("bst,bsd->btd", sel, vals, preferred_element_type=f32).astype(bf16)
        return lax.psum_scatter(part.reshape(ranks * rows, width), "expert", scatter_dimension=0, tiled=True)

    x_rows = to_slots(pick, x_all)
    pre_gate = jnp.einsum("erd,edf->erf", x_rows, w_gate, preferred_element_type=f32)
    pre_up = jnp.einsum("erd,edf->erf", x_rows, w_up, preferred_element_type=f32)
    sig = jax.nn.sigmoid(pre_gate)
    act = pre_gate * sig
    hidden = (act * pre_up).astype(bf16)
    expert_out = jnp.einsum("erf,efd->erd", hidden, w_down, preferred_element_type=f32).astype(bf16)
    output = from_slots(pick_w, expert_out)
    do_rows = to_slots(pick_w, c_all)
    hidden_grad = jnp.einsum("erd,efd->erf", do_rows, w_down, preferred_element_type=f32)
    gate_grad = (hidden_grad * pre_up * sig * (1.0 + pre_gate * (1.0 - sig))).astype(bf16)
    up_grad = (hidden_grad * act).astype(bf16)
    pick_grad = (
        jnp.einsum("erf,edf->erd", gate_grad, w_gate, preferred_element_type=f32)
        + jnp.einsum("erf,edf->erd", up_grad, w_up, preferred_element_type=f32)
    ).astype(bf16)
    tokens_grad = from_slots(pick, pick_grad)
    down_part = jnp.einsum("erf,erd->efd", hidden, do_rows, preferred_element_type=f32)
    gate_part = jnp.einsum("erd,erf->edf", x_rows, gate_grad, preferred_element_type=f32)
    up_part = jnp.einsum("erd,erf->edf", x_rows, up_grad, preferred_element_type=f32)
    down_total = lax.psum_scatter(down_part.astype(bf16), "dp", scatter_dimension=2, tiled=True)
    gate_total = lax.psum_scatter(gate_part.astype(bf16), "dp", scatter_dimension=1, tiled=True)
    up_total = lax.psum_scatter(up_part.astype(bf16), "dp", scatter_dimension=1, tiled=True)
    return output, tokens_grad, gate_total, up_total, down_total


def solution(mesh):
    in_specs = (
        P(("dp", "expert"), None),
        P(("dp", "expert"), None),
        P(("dp", "expert"), None),
        P("expert", None, None),
        P("expert", None, None),
        P("expert", None, None),
        P(("dp", "expert"), None),
    )
    out_specs = (
        P(("dp", "expert"), None),
        P(("dp", "expert"), None),
        P("expert", "dp", None),
        P("expert", "dp", None),
        P("expert", None, "dp"),
    )
    return jax.shard_map(local, mesh=mesh, in_specs=in_specs, out_specs=out_specs, check_vma=False)
```

profile of v0, /device:TPU:0, one launch (start us, length us, event | category | flops | bytes accessed | tf_op | source)
XLA Modules:
  0.0 394.8 jit_solution(17007096960214568542)
XLA Ops:
  9.5 32.4 %all-gather = s32[1024,8]{0,1:T(8,128)S(1)} all-gather(s32[128,8]{0,1:T(8,128)S(1)} %multiply_add_fusion), channel_id=2, replica_groups=mesh['dp'=4,'expert'=8] {'expert'}, dimensions={0}, use_global_device_ids=true | all-gather | bytes 36864 | tf_op jit(solution)/shard_map/all_gather | solution.py:17
  42.3 0.8 bitcast_compare_fusion
  43.4 18.9 %all-gather.8.cloned.1.call-done = bf16[1024,1024]{1,0:T(8,128)(2,1)} async-done(((bf16[128,1024]{1,0:T(8,128)(2,1)}), bf16[1024,1024]{1,0:T(8,128)(2,1)}) %all-gather.8.cloned.1.call-update) | async-done | bytes 2097168 | tf_op jit(solution)/shard_map/all_gather | solution.py:19
  62.3 2.4 convolution_convert_fusion.4
  64.7 1.8 copy.24
  66.5 45.7 %all-gather.6.cloned.1.call-done = bf16[1024,1024]{1,0:T(8,128)(2,1)} async-done(((bf16[128,1024]{1,0:T(8,128)(2,1)}), bf16[1024,1024]{1,0:T(8,128)(2,1)}) %all-gather.6.cloned.1.call-update) | async-done | bytes 2097168 | tf_op jit(solution)/shard_map/all_gather | solution.py:18
  112.3 2.5 convolution_convert_fusion.3
  115.1 2.5 copy-done.3
  117.6 1.5 fusion.17
  119.5 1.6 fusion.16
  121.3 3.5 multiply_convert_fusion
  124.7 1.5 convolution_convert_fusion.5
  126.6 2.1 convolution_convert_fusion.7
  129.0 3.9 fusion.18
  132.9 1.6 add_convert_fusion
  135.4 2.1 convolution_convert_fusion.6
  137.6 5.5 %convolution_convert_fusion = bf16[4,384,1024]{2,1,0:T(8,128)(2,1)} fusion(bf16[4,320,384]{2,1,0:T(8,128)(2,1)} %copy-done.6, bf16[4,320,1024]{2,1,0:T(8,128)(2,1)} %bitcast.92), kind=kOutput, calls=%fused_computation.1 | convolution fusion | flops 1008205824 | bytes 6750208 | tf_op jit(solution)/shard_map/erf,erd->efd/dot_general | solution.py:64
  143.2 5.8 %convolution_convert_fusion.1 = bf16[4,1024,384]{2,1,0:T(8,128)(2,1)} fusion(bf16[4,320,1024]{2,1,0:T(8,128)(2,1)} %bitcast.89, bf16[4,320,384]{2,1,0:T(8,128)(2,1)} %get-tuple-element.5), kind=kOutput, calls=%fused_computation.2 | convolution fusion | flops 1008205824 | bytes 6750208 | tf_op jit(solution)/shard_map/erd,erf->edf/dot_general | solution.py:66
  149.1 5.8 %convolution_convert_fusion.2 = bf16[4,1024,384]{2,1,0:T(8,128)(2,1)} fusion(bf16[4,320,1024]{2,1,0:T(8,128)(2,1)} %bitcast.90, bf16[4,320,384]{2,1,0:T(8,128)(2,1)} %get-tuple-element.6), kind=kOutput, calls=%fused_computation.3 | convolution fusion | flops 1008205824 | bytes 6750208 | tf_op jit(solution)/shard_map/erd,erf->edf/dot_general | solution.py:65
  154.9 40.0 %reduce-scatter.6.cloned.1.call-done = bf16[128,1024]{1,0:T(8,128)(2,1)} async-done(((bf16[1024,1024]{1,0:T(8,128)(2,1)}), bf16[128,1024]{1,0:T(8,128)(2,1)}) %reduce-scatter.6.cloned.1.call-update) | async-done | bytes 262160 | tf_op jit(solution)/shard_map/reduce_scatter | solution.py:45
  194.9 70.8 %reduce-scatter.8.cloned.1.call-done = bf16[128,1024]{1,0:T(8,128)(2,1)} async-done(((bf16[1024,1024]{1,0:T(8,128)(2,1)}), bf16[128,1024]{1,0:T(8,128)(2,1)}) %reduce-scatter.8.cloned.1.call-update) | async-done | bytes 262160 | tf_op jit(solution)/shard_map/reduce_scatter | solution.py:45
  265.7 40.1 %reduce-scatter.14.cloned.1.call-done = bf16[4,384,256]{2,1,0:T(8,128)(2,1)} async-done(((bf16[4,384,1024]{2,1,0:T(8,128)(2,1)}), bf16[4,384,256]{2,1,0:T(8,128)(2,1)}) %reduce-scatter.14.cloned.1.call-update) | async-done | bytes 786448 | tf_op jit(solution)/shard_map/reduce_scatter | solution.py:67
  305.8 41.1 %reduce-scatter.12.cloned.1.call-done = bf16[4,256,384]{2,1,0:T(8,128)(2,1)} async-done(((bf16[4,1024,384]{2,1,0:T(8,128)(2,1)}), bf16[4,256,384]{2,1,0:T(8,128)(2,1)}) %reduce-scatter.12.cloned.1.call-update) | async-done | bytes 786448 | tf_op jit(solution)/shard_map/reduce_scatter | solution.py:69
  346.9 41.1 %reduce-scatter.10.cloned.1.call-done = bf16[4,256,384]{2,1,0:T(8,128)(2,1)} async-done(((bf16[4,1024,384]{2,1,0:T(8,128)(2,1)}), bf16[4,256,384]{2,1,0:T(8,128)(2,1)}) %reduce-scatter.10.cloned.1.call-update) | async-done | bytes 786448 | tf_op jit(solution)/shard_map/reduce_scatter | solution.py:68
  (46 shorter events, 5.4 us)
Async XLA Ops:
  7.2 113.9 %copy-start = (bf16[4,384,1024]{2,1,0:T(8,128)(2,1)S(1)}, bf16[4,384,1024]{2,1,0:T(8,128)(2,1)}, u32[]{:S(2)}) copy-start(bf16[4,384,1024]{2,1,0:T(8,128)(2,1)} %param.12) | copy-start | bytes 9437188
  7.2 55.1 %all-gather.8.cloned.1.call-start = ((), (), s32[]{:S(2)}) async-start(), calls=%async_computation.11 | async-start | bytes 2359296 | tf_op jit(solution)/shard_map/all_gather | solution.py:19
  7.9 104.3 %all-gather.6.cloned.1.call-start = ((), (), s32[]{:S(2)}) async-start(), calls=%async_computation.10 | async-start | bytes 2359296 | tf_op jit(solution)/shard_map/all_gather | solution.py:18
  8.7 186.3 %reduce-scatter.6.cloned.1.call-start = ((), (), s32[]{:S(2)}) async-start(), calls=%async_computation.5 | async-start | bytes 2359296 | tf_op jit(solution)/shard_map/reduce_scatter | solution.py:45
  114.8 2.8 copy-start.3
  115.1 4.0 %copy-start.1 = (bf16[4,8,40,1024]{3,2,1,0:T(8,128)(2,1)}, bf16[4,8,40,1024]{3,2,1,0:T(8,128)(2,1)S(1)}, u32[]{:S(2)}) copy-start(bf16[4,8,40,1024]{3,2,1,0:T(8,128)(2,1)S(1)} %copy.22) | copy-start | bytes 7864324
  117.6 1.9 copy-start.2
  119.5 1.7 copy-start.5
  124.7 1.6 copy-start.6
  128.8 136.9 %reduce-scatter.8.cloned.1.call-start = ((), (), s32[]{:S(2)}) async-start(), calls=%async_computation.6 | async-start | bytes 2359296 | tf_op jit(solution)/shard_map/reduce_scatter | solution.py:45
  129.0 3.9 copy-start.4
  129.0 3.9 copy-start.7
  134.5 0.9 copy-start.8
  137.5 168.2 %reduce-scatter.14.cloned.1.call-start = ((), (), s32[]{:S(2)}) async-start(), calls=%async_computation.9 | async-start | bytes 3932160 | tf_op jit(solution)/shard_map/reduce_scatter | solution.py:67
  143.1 203.8 %reduce-scatter.12.cloned.1.call-start = ((), (), s32[]{:S(2)}) async-start(), calls=%async_computation.8 | async-start | bytes 3932160 | tf_op jit(solution)/shard_map/reduce_scatter | solution.py:69
  149.0 239.0 %reduce-scatter.10.cloned.1.call-start = ((), (), s32[]{:S(2)}) async-start(), calls=%async_computation.7 | async-start | bytes 3932160 | tf_op jit(solution)/shard_map/reduce_scatter | solution.py:68
Sparse Core Ops, SparseCore 0:
  10.1 52.1 all-gather.7
  64.4 47.7 all-gather.5
  128.9 65.9 reduce-scatter.5
  198.9 66.7 reduce-scatter.7
  268.6 37.0 reduce-scatter.13
  308.9 37.9 reduce-scatter.11
  350.0 37.9 reduce-scatter.9
where the time goes:
time: 395 us
  waiting for transfers between devices  299 us (76%)
  matrix products  40 us (10%)
  blocking collectives  32.4 us (8%)
  between operations  14.3 us (4%)
  local copies, waits for them, and re-layouts  6.48 us (2%)
    reduce_scatter x2, waiting for transfers between devices, from_slots(): lax.psum_scatter(part.reshape(ranks * rows, width), 'expert', scatter_dim...  111 us
    all_gather x1, waiting for transfers between devices, local(): x_all = lax.all_gather(tokens, 'expert')  45.7 us
    reduce_scatter x1, waiting for transfers between devices, local(): lax.psum_scatter(up_part.astype(bf16), 'dp', scatter_dimension=1, tiled=T...  41.1 us
    reduce_scatter x1, waiting for transfers between devices, local(): lax.psum_scatter(gate_part.astype(bf16), 'dp', scatter_dimension=1, tiled...  41.1 us
    reduce_scatter x1, waiting for transfers between devices, local(): lax.psum_scatter(down_part.astype(bf16), 'dp', scatter_dimension=2, tiled...  40.1 us
    all_gather x1, blocking collectives, local(): packed = lax.all_gather(expert_ids * 512 + route_num, 'expert')  32.4 us
    all_gather x1, waiting for transfers between devices, local(): c_all = lax.all_gather(cotangent, 'expert')  18.9 us
  transfers between devices with their start and end apart: 7, of which 7 were waited for; matrix products, arithmetic and copies ran while one was open for 8% of the time, Pallas kernels for 0%

commit v1 on v0

--- a/solution.py
+++ b/solution.py
@@ -1,9 +1,228 @@
+import functools
+
 import jax
 import jax.numpy as jnp
 from jax import lax
+from jax.experimental import pallas as pl
+from jax.experimental.pallas import tpu as pltpu
 from jax.sharding import PartitionSpec as P
 
 DENOM = 256
+MESH = pl.DeviceIdType.MESH
+ANY = pl.BlockSpec(memory_space=pl.ANY)
+VMEM = pl.BlockSpec(memory_space=pltpu.VMEM)
+
+
+def greet(axes):
+    barrier = pltpu.get_barrier_semaphore()
+    count = 0
+    for axis, size in axes:
+        major, minor, groups = split_index(axis, size)
+        peers = [2 * major + 1 - minor]
+        peers += [2 * lax.rem(major + k, groups) + minor for k in range(1, groups)]
+        for peer in peers:
+            pl.semaphore_signal(barrier, inc=1, device_id={axis: peer}, device_id_type=MESH)
+        count += len(peers)
+    pl.semaphore_wait(barrier, count)
+
+
+def split_index(axis, size):
+    me = lax.axis_index(axis)
+    return me // 2, lax.rem(me, 2), size // 2
+
+
+def gather_kernel(ranks, *refs):
+    srcs, outs, (send, recv, local_sem) = refs[:3], refs[3:6], refs[6:]
+    major, minor, groups = split_index("expert", ranks)
+    me = 2 * major + minor
+    partner = 2 * major + 1 - minor
+    greet([("expert", ranks)])
+    copies = []
+
+    def push(t, src, shard, slot, peer):
+        copy = pltpu.make_async_remote_copy(
+            src_ref=src, dst_ref=outs[t].at[shard], send_sem=send.at[t, slot], recv_sem=recv.at[t, shard],
+            device_id={"expert": peer}, device_id_type=MESH,
+        )
+        copy.start()
+        copies.append(copy)
+
+    def arrived(t, shard):
+        pltpu.make_async_remote_copy(
+            src_ref=outs[t].at[shard], dst_ref=outs[t].at[shard], send_sem=send.at[t, 0], recv_sem=recv.at[t, shard],
+            device_id={"expert": partner}, device_id_type=MESH,
+        ).wait_recv()
+
+    for t in range(3):
+        push(t, srcs[t], me, 0, partner)
+        for k in range(1, groups):
+            push(t, srcs[t], me, k, 2 * lax.rem(major + k, groups) + minor)
+    keep = [pltpu.make_async_copy(srcs[t], outs[t].at[me], local_sem.at[t]) for t in range(3)]
+    for copy in keep:
+        copy.start()
+    for t in range(3):
+        for k in range(1, groups):
+            shard = 2 * lax.rem(major - k + groups, groups) + minor
+            arrived(t, shard)
+            push(t, outs[t].at[shard], shard, groups + k - 1, partner)
+    for t in range(3):
+        for k in range(groups):
+            arrived(t, 2 * lax.rem(major - k + groups, groups) + 1 - minor)
+    for copy in copies:
+        copy.wait_send()
+    for copy in keep:
+        copy.wait()
+
+
+def gather(ranks, packed, tokens, cotangent):
+    srcs = (packed, tokens, cotangent)
+    return pl.pallas_call(
+        functools.partial(gather_kernel, ranks),
+        out_shape=[jax.ShapeDtypeStruct((ranks, *a.shape), a.dtype) for a in srcs],
+        in_specs=[ANY] * 3,
+        out_specs=[ANY] * 3,
+        scratch_shapes=[
+            pltpu.SemaphoreType.DMA((3, ranks)),
+            pltpu.SemaphoreType.DMA((3, ranks)),
+            pltpu.SemaphoreType.DMA((3,)),
+        ],
+        compiler_params=pltpu.CompilerParams(collective_id=0, has_side_effects=True),
+    )(*srcs)
+
+
+class Job:
+    def __init__(self, axis, size, source, land, stage, got, sems):
+        self.axis, self.source, self.land, self.stage, self.got = axis, source, land, stage, got
+        self.s1, self.r1, self.s2, self.r2, self.ls = sems
+        self.major, self.minor, self.groups = split_index(axis, size)
+        self.partner = 2 * self.major + 1 - self.minor
+        self.copies = []
+
+    def remote(self, src, dst, s, r, peer):
+        return pltpu.make_async_remote_copy(
+            src_ref=src, dst_ref=dst, send_sem=s, recv_sem=r, device_id={self.axis: peer}, device_id_type=MESH
+        )
+
+    def target(self, k):
+        return lax.rem(self.major + k, self.groups)
+
+    def order(self):
+        return list(range(1, self.groups)) + [0]
+
+    def exchange(self):
+        for k in self.order():
+            to = self.target(k)
+            copy = self.remote(
+                self.source(2 * to + 1 - self.minor), self.land.at[k], self.s1.at[k], self.r1.at[k], self.partner
+            )
+            copy.start()
+            self.copies.append(copy)
+            pltpu.make_async_copy(self.source(2 * to + self.minor), self.stage.at[k], self.ls.at[k]).start()
+
+    def pair_sum(self, k):
+        pltpu.make_async_copy(self.source(2 * self.target(k) + self.minor), self.stage.at[k], self.ls.at[k]).wait()
+        self.remote(self.land.at[k], self.land.at[k], self.s1.at[k], self.r1.at[k], self.partner).wait_recv()
+        total = self.stage[k].astype(jnp.float32) + self.land[k].astype(jnp.float32)
+        self.stage[k] = total.astype(jnp.bfloat16)
+        if k:
+            copy = self.remote(
+                self.stage.at[k], self.got.at[k - 1], self.s2.at[k - 1], self.r2.at[k - 1],
+                2 * self.target(k) + self.minor,
+            )
+            copy.start()
+            self.copies.append(copy)
+
+    def finish(self):
+        total = self.stage[0].astype(jnp.float32)
+        for k in range(1, self.groups):
+            slot = self.got.at[k - 1]
+            self.remote(slot, slot, self.s2.at[k - 1], self.r2.at[k - 1], self.partner).wait_recv()
+            total = total + self.got[k - 1].astype(jnp.float32)
+        return total.astype(jnp.bfloat16)
+
+    def drain(self):
+        for copy in self.copies:
+            copy.wait_send()
+
+
+def reduce_kernel(ranks, groups_dp, exp_dev, *refs):
+    (part_o, part_t, part_g, part_u, part_d), refs = refs[:5], refs[5:]
+    (out_o, out_t, out_g, out_u, out_d), refs = refs[:5], refs[5:]
+    (land_e, stage_e, got_e, land_w, stage_w, got_w, land_d, stage_d, got_d), refs = refs[:9], refs[9:]
+    sems_e, sems_w = refs[:5], refs[5:10]
+    span = out_g.shape[1]
+    greet([("expert", ranks), ("dp", groups_dp)])
+    tok_jobs = [
+        Job("expert", ranks, lambda i, p=p: p.at[i], land_e.at[j], stage_e.at[j], got_e.at[j], [s.at[j] for s in sems_e])
+        for j, p in enumerate((part_o, part_t))
+    ]
+    w_jobs = []
+    for e in range(exp_dev):
+        for j, p in enumerate((part_g, part_u)):
+            w_jobs.append(Job(
+                "dp", groups_dp, lambda i, p=p, e=e: p.at[e, pl.ds(pl.multiple_of(i * span, span), span), :],
+                land_w.at[j, e], stage_w.at[j, e], got_w.at[j, e], [s.at[j, e] for s in sems_w],
+            ))
+        w_jobs.append(Job(
+            "dp", groups_dp, lambda i, e=e: part_d.at[e, :, pl.ds(pl.multiple_of(i * span, span), span)],
+            land_d.at[e], stage_d.at[e], got_d.at[e], [s.at[2, e] for s in sems_w],
+        ))
+    for job in tok_jobs + w_jobs:
+        job.exchange()
+    todo_t = [(job, k) for job in tok_jobs for k in job.order()]
+    todo_w = [(job, k) for k in w_jobs[0].order() for job in w_jobs]
+    while todo_t or todo_w:
+        for todo in (todo_w, todo_t):
+            if todo:
+                job, k = todo.pop(0)
+                job.pair_sum(k)
+    out_o[...] = tok_jobs[0].finish()
+    out_t[...] = tok_jobs[1].finish()
+    for n, job in enumerate(w_jobs):
+        (out_g, out_u, out_d)[n % 3][n // 3] = job.finish()
+    for job in tok_jobs + w_jobs:
+        job.drain()
+
+
+def reduce_all(ranks, groups_dp, part_o, part_t, part_g, part_u, part_d):
+    bf16 = jnp.bfloat16
+    exp_dev, width, hid = part_g.shape
+    rows = part_o.shape[1]
+    span = width // groups_dp
+    m_e, m_d = ranks // 2, groups_dp // 2
+
+    def slots(lead, block, groups):
+        return [
+            pltpu.VMEM((*lead, groups, *block), bf16),
+            pltpu.VMEM((*lead, groups, *block), bf16),
+            pltpu.VMEM((*lead, groups - 1, *block), bf16),
+        ]
+
+    def sems(lead, groups):
+        return [pltpu.SemaphoreType.DMA((*lead, groups)) for _ in range(5)]
+
+    return pl.pallas_call(
+        functools.partial(reduce_kernel, ranks, groups_dp, exp_dev),
+        out_shape=[
+            jax.ShapeDtypeStruct((rows, width), bf16),
+            jax.ShapeDtypeStruct((rows, width), bf16),
+            jax.ShapeDtypeStruct((exp_dev, span, hid), bf16),
+            jax.ShapeDtypeStruct((exp_dev, span, hid), bf16),
+            jax.ShapeDtypeStruct((exp_dev, hid, span), bf16),
+        ],
+        in_specs=[ANY] * 5,
+        out_specs=[VMEM] * 5,
+        scratch_shapes=[
+            *slots((2,), (rows, width), m_e),
+            *slots((2, exp_dev), (span, hid), m_d),
+            *slots((exp_dev,), (hid, span), m_d),
+            *sems((2,), m_e),
+            *sems((3, exp_dev), m_d),
+        ],
+        compiler_params=pltpu.CompilerParams(
+            collective_id=1, has_side_effects=True, vmem_limit_bytes=56 * 1024 * 1024
+        ),
+    )(part_o, part_t, part_g, part_u, part_d)
 
 
 def local(tokens, expert_ids, route_num, w_gate, w_up, w_down, cotangent):
@@ -14,9 +233,8 @@
     capacity = 5 * rows // 16
     bf16, f32 = jnp.bfloat16, jnp.float32
 
-    packed = lax.all_gather(expert_ids * 512 + route_num, "expert")
-    x_all = lax.all_gather(tokens, "expert")
-    c_all = lax.all_gather(cotangent, "expert")
+    packed, x_all, c_all = gather(ranks, (expert_ids * 512 + route_num).T, tokens, cotangent)
+    packed = packed.transpose(0, 2, 1)
 
     ids, num = packed // 512, packed % 512
     first = lax.axis_index("expert") * exp_dev
@@ -42,7 +260,7 @@
         vals = vals.reshape(exp_dev, ranks, capacity, width).transpose(1, 0, 2, 3)
         vals = vals.reshape(ranks, exp_dev * capacity, width)
         part = jnp.einsum("bst,bsd->btd", sel, vals, preferred_element_type=f32).astype(bf16)
-        return lax.psum_scatter(part.reshape(ranks * rows, width), "expert", scatter_dimension=0, tiled=True)
+        return part
 
     x_rows = to_slots(pick, x_all)
     pre_gate = jnp.einsum("erd,edf->erf", x_rows, w_gate, preferred_element_type=f32)
@@ -51,7 +269,7 @@
     act = pre_gate * sig
     hidden = (act * pre_up).astype(bf16)
     expert_out = jnp.einsum("erf,efd->erd", hidden, w_down, preferred_element_type=f32).astype(bf16)
-    output = from_slots(pick_w, expert_out)
+    out_part = from_slots(pick_w, expert_out)
     do_rows = to_slots(pick_w, c_all)
     hidden_grad = jnp.einsum("erd,efd->erf", do_rows, w_down, preferred_element_type=f32)
     gate_grad = (hidden_grad * pre_up * sig * (1.0 + pre_gate * (1.0 - sig))).astype(bf16)
@@ -60,14 +278,14 @@
         jnp.einsum("erf,edf->erd", gate_grad, w_gate, preferred_element_type=f32)
         + jnp.einsum("erf,edf->erd", up_grad, w_up, preferred_element_type=f32)
     ).astype(bf16)
-    tokens_grad = from_slots(pick, pick_grad)
+    grad_part = from_slots(pick, pick_grad)
     down_part = jnp.einsum("erf,erd->efd", hidden, do_rows, preferred_element_type=f32)
     gate_part = jnp.einsum("erd,erf->edf", x_rows, gate_grad, preferred_element_type=f32)
     up_part = jnp.einsum("erd,erf->edf", x_rows, up_grad, preferred_element_type=f32)
-    down_total = lax.psum_scatter(down_part.astype(bf16), "dp", scatter_dimension=2, tiled=True)
-    gate_total = lax.psum_scatter(gate_part.astype(bf16), "dp", scatter_dimension=1, tiled=True)
-    up_total = lax.psum_scatter(up_part.astype(bf16), "dp", scatter_dimension=1, tiled=True)
-    return output, tokens_grad, gate_total, up_total, down_total
+    return tuple(reduce_all(
+        ranks, lax.axis_size("dp"), out_part, grad_part,
+        gate_part.astype(bf16), up_part.astype(bf16), down_part.astype(bf16),
+    ))
 
 
 def solution(mesh):

time: 395 us -> 179 us (0.45)
  waiting for transfers between devices: 299 us -> 0 us
  Pallas kernels: 0 us -> 134 us
  blocking collectives: 32.4 us -> 0 us
  between operations: 14.3 us -> 0.86 us
  matrix products: 40 us -> 28.8 us
  local copies, waits for them, and re-layouts: 6.48 us -> 11.6 us
    reduce_scatter x5 -> x0, waiting for transfers between devices: 233 us -> none  [the longest x2 111 us: from_slots(): lax.psum_scatter(part.reshape(ranks * rows, width), 'expert', scatter_dim...]
    pallas_call x0 -> x2, Pallas kernels: none -> 134 us  [the longest x1 73.7 us: reduce_all(): pl.pallas_call(functools.partial(reduce_kernel, ranks, groups_dp, exp_dev...]
    all_gather x2 -> x0, waiting for transfers between devices: 64.6 us -> none  [the longest x1 45.7 us: local(): x_all = lax.all_gather(tokens, 'expert')]
    all_gather x1 -> x0, blocking collectives: 32.4 us -> none  [local(): packed = lax.all_gather(expert_ids * 512 + route_num, 'expert')]
    unnamed x18 -> x17, local copies, waits for them, and re-layouts: 3.69 us -> 10.4 us
  transfers between devices with their start and end apart: 7 -> 0, of which waited for: 7 -> 0; matrix products, arithmetic and copies ran while one was open for 8% -> 0% of each run, Pallas kernels for 0% -> 0%
where the time goes in v1:
time: 179 us; the launch traced here: 178 us
  Pallas kernels  134 us (75%)
  matrix products  28.8 us (16%)
  local copies, waits for them, and re-layouts  11.6 us (6%)
  other arithmetic  2.79 us (2%)
    pallas_call x1, Pallas kernels, reduce_all(): pl.pallas_call(functools.partial(reduce_kernel, ranks, groups_dp, exp_dev...  73.7 us
    pallas_call x1, Pallas kernels, gather(): pl.pallas_call(functools.partial(gather_kernel, ranks), out_shape=[jax.Sh...  60.5 us
    unnamed x17, local copies, waits for them, and re-layouts  10.4 us
    dot_general x2, matrix products, from_slots(): jnp.einsum('bst,bsd->btd', sel, vals, preferred_element_type=f32)  4.24 us
    dot_general x1, matrix products, local(): jnp.einsum('erd,erf->edf', x_rows, up_grad, preferred_element_type=f32)  3.81 us
    dot_general x1, matrix products, local(): jnp.einsum('erd,erf->edf', x_rows, gate_grad, preferred_element_type=f32)  3.78 us

profile of v1, /device:TPU:0, one launch (start us, length us, event | category | flops | bytes accessed | tf_op | source)
XLA Modules:
  0.0 178.2 jit_solution(17965300107016979894)
XLA Ops:
  0.6 1.4 add_bitcast_fusion.refs_0_
  2.1 60.5 %shard_map.110 = (s32[8,8,128]{2,1,0:T(8,128)}, bf16[8,128,1024]{2,1,0:T(8,128)(2,1)}, bf16[8,128,1024]{2,1,0:T(8,128)(2,1)}) custom-call(s32[8,128]{1,0:T(8,128)} %add_bitcast_fusion.refs_0_, bf16[128,1024]{1,0:T(8,128)(2,1)} %refs_1_.1, bf16[128,1024]{1,0:T(8,128)(2,1)} %refs_2_.1), custom_call_target="tpu_custom_call" | custom-call | tf_op jit(solution)/shard_map/pallas_call | solution.py:79
  62.6 0.8 add_select_fusion.1
  64.1 2.4 %convolution_convert_fusion.4 = bf16[8,160,1024]{2,1,0:T(8,128)(2,1)S(1)} fusion(bf16[8,160,128]{2,1,0:T(8,128)(2,1)S(1)} %fusion.2, bf16[8,128,1024]{2,1,0:T(8,128)(2,1)} %get-tuple-element.10), kind=kOutput, calls=%fused_computation.5 | convolution fusion | flops 336855040 | bytes 5046272 | tf_op jit(solution)/shard_map/bst,btd->bsd/dot_general | solution.py:255
  67.0 1.1 copy-done.3
  68.1 0.8 convolution_convert_fusion.3
  69.3 1.6 copy-done.1
  70.9 1.5 fusion.16
  72.7 1.5 fusion.17
  74.3 2.1 %multiply_convert_fusion = (bf16[4,320,384]{2,1,0:T(8,128)(2,1)S(1)}, bf16[4,320,384]{2,1,0:T(8,128)(2,1)S(1)}, bf16[4,320,384]{2,1,0:T(8,128)(2,1)S(1)}) fusion(f32[4,320,384]{2,1,0:T(8,128)S(1)} %fusion.16, f32[4,320,384]{2,1,0:T(8,128)S(1)} %fusion.17, bf16[4,320,1024]{2,1,0:T(8,128)(2,1)S(1)} %bitcast.90, bf16[4,384,1024]{2,1,0:T(8,128)(2,1)S(1)} %copy-done), kind=kOutput, calls=%fused_computation.7 | convolution fusion | flops 1014005760 | bytes 12648448 | tf_op jit(solution)/shard_map/erd,efd->erf/dot_general | solution.py:274
  76.4 1.5 fusion.18
  78.0 1.6 add_convert_fusion
  79.8 2.2 %convolution_convert_fusion.6.refs_1_ = bf16[8,128,1024]{2,1,0:T(8,128)(2,1)} fusion(pred[8,160,128]{2,1,0:T(32,128)(4,1)S(1)} %bitcast_compare_fusion, bf16[8,160,1024]{2,1,0:T(8,128)(2,1)S(1)} %bitcast.92), kind=kOutput, calls=%fused_computation.12 | convolution fusion | flops 336592896 | bytes 4882432 | tf_op jit(solution)/shard_map/bst,bsd->btd/dot_general | solution.py:262
  82.0 3.5 %convolution_convert_fusion.refs_4_ = bf16[4,384,1024]{2,1,0:T(8,128)(2,1)} fusion(bf16[4,320,384]{2,1,0:T(8,128)(2,1)S(1)} %get-tuple-element.13, bf16[4,320,1024]{2,1,0:T(8,128)(2,1)S(1)} %bitcast.91), kind=kOutput, calls=%fused_computation.1 | convolution fusion | flops 1008205824 | bytes 6750208 | tf_op jit(solution)/shard_map/erf,erd->efd/dot_general | solution.py:282
  85.5 1.7 convolution_convert_fusion.5
  87.5 2.1 %convolution_convert_fusion.7.refs_0_ = bf16[8,128,1024]{2,1,0:T(8,128)(2,1)} fusion(bf16[8,160,128]{2,1,0:T(8,128)(2,1)S(1)} %fusion.2, bf16[8,160,1024]{2,1,0:T(8,128)(2,1)S(1)} %bitcast.93), kind=kOutput, calls=%fused_computation.13 | convolution fusion | flops 336592896 | bytes 5046272 | tf_op jit(solution)/shard_map/bst,bsd->btd/dot_general | solution.py:262
  89.6 3.8 %convolution_convert_fusion.1.refs_3_ = bf16[4,1024,384]{2,1,0:T(8,128)(2,1)} fusion(bf16[4,320,1024]{2,1,0:T(8,128)(2,1)S(1)} %bitcast.87, bf16[4,320,384]{2,1,0:T(8,128)(2,1)S(1)} %get-tuple-element.11), kind=kOutput, calls=%fused_computation.2 | convolution fusion | flops 1008205824 | bytes 6750208 | tf_op jit(solution)/shard_map/erd,erf->edf/dot_general | solution.py:284
  93.4 3.8 %convolution_convert_fusion.2.refs_2_ = bf16[4,1024,384]{2,1,0:T(8,128)(2,1)} fusion(bf16[4,320,1024]{2,1,0:T(8,128)(2,1)S(1)} %bitcast.88, bf16[4,320,384]{2,1,0:T(8,128)(2,1)S(1)} %get-tuple-element.12), kind=kOutput, calls=%fused_computation.3 | convolution fusion | flops 1008205824 | bytes 6750208 | tf_op jit(solution)/shard_map/erd,erf->edf/dot_general | solution.py:283
  97.2 73.7 %shard_map.111 = (bf16[128,1024]{1,0:T(8,128)(2,1)}, bf16[128,1024]{1,0:T(8,128)(2,1)}, bf16[4,256,384]{2,1,0:T(8,128)(2,1)}, bf16[4,256,384]{2,1,0:T(8,128)(2,1)}, bf16[4,384,256]{2,1,0:T(8,128)(2,1)}) custom-call(bf16[8,128,1024]{2,1,0:T(8,128)(2,1)} %convolution_convert_fusion.7.refs_0_, bf16[8,128,1024]{2,1,0:T(8,128)(2,1)} %convolution_convert_fusion.6.refs_1_, ...), custom_call_target="tpu_custom_call" | custom-call | tf_op jit(solution)/shard_map/pallas_call | solution.py:204
  170.9 1.8 %copy.36 = bf16[128,1024]{1,0:T(8,128)(2,1)} copy(bf16[128,1024]{1,0:T(8,128)(2,1)} %get-tuple-element.21) | data formatting | bytes 524288
  172.7 1.7 copy.37
  174.3 2.1 %copy.38 = bf16[4,256,384]{2,1,0:T(8,128)(2,1)} copy(bf16[4,256,384]{2,1,0:T(8,128)(2,1)} %get-tuple-element.23) | data formatting | bytes 1572864
  176.4 0.9 copy.39
  177.3 0.9 copy.40
  (25 shorter events, 2.4 us)
Async XLA Ops:
  0.6 73.6 %copy-start = (bf16[4,384,1024]{2,1,0:T(8,128)(2,1)S(1)}, bf16[4,384,1024]{2,1,0:T(8,128)(2,1)}, u32[]{:S(2)}) copy-start(bf16[4,384,1024]{2,1,0:T(8,128)(2,1)} %param.12) | copy-start | bytes 9437188
  66.5 1.6 copy-start.3
  69.0 1.9 %copy-start.1 = (bf16[4,1024,384]{2,1,0:T(8,128)(2,1)S(1)}, bf16[4,1024,384]{2,1,0:T(8,128)(2,1)}, u32[]{:S(2)}) copy-start(bf16[4,1024,384]{2,1,0:T(8,128)(2,1)} %param.10) | copy-start | bytes 9437188
  70.9 1.9 %copy-start.2 = (bf16[4,1024,384]{2,1,0:T(8,128)(2,1)S(1)}, bf16[4,1024,384]{2,1,0:T(8,128)(2,1)}, u32[]{:S(2)}) copy-start(bf16[4,1024,384]{2,1,0:T(8,128)(2,1)} %param.11) | copy-start | bytes 9437188
  170.9 5.6 %copy-start.5 = (bf16[4,256,384]{2,1,0:T(8,128)(2,1)S(1)}, bf16[4,256,384]{2,1,0:T(8,128)(2,1)}, u32[]{:S(2)}) copy-start(bf16[4,256,384]{2,1,0:T(8,128)(2,1)} %get-tuple-element.24) | copy-start | bytes 2359300
  170.9 6.4 %copy-start.4 = (bf16[4,384,256]{2,1,0:T(8,128)(2,1)S(1)}, bf16[4,384,256]{2,1,0:T(8,128)(2,1)}, u32[]{:S(2)}) copy-start(bf16[4,384,256]{2,1,0:T(8,128)(2,1)} %get-tuple-element.25) | copy-start | bytes 2359300

commit v2 on v0

v2 whole, which is shorter than its diff:
```python
import functools

import jax
import jax.numpy as jnp
from jax import lax
from jax.experimental import pallas as pl
from jax.experimental.pallas import tpu as pltpu
from jax.sharding import PartitionSpec as P

DENOM = 256
MESH = pl.DeviceIdType.MESH
ANY = pl.BlockSpec(memory_space=pl.ANY)
VMEM = pl.BlockSpec(memory_space=pltpu.VMEM)
BF16, F32 = jnp.bfloat16, jnp.float32


def split_index(axis, size):
    me = lax.axis_index(axis)
    return me // 2, lax.rem(me, 2), size // 2


def greet(axes):
    barrier = pltpu.get_barrier_semaphore()
    count = 0
    for axis, size in axes:
        major, minor, groups = split_index(axis, size)
        peers = [2 * major + 1 - minor]
        peers += [2 * lax.rem(major + k, groups) + minor for k in range(1, groups)]
        for peer in peers:
            pl.semaphore_signal(barrier, inc=1, device_id={axis: peer}, device_id_type=MESH)
        count += len(peers)
    pl.semaphore_wait(barrier, count)


def dot(a, b, ca, cb):
    return lax.dot_general(a, b, (((ca,), (cb,)), ((), ())), preferred_element_type=F32)


class Gather:
    def __init__(self, ranks, src, out, send, recv, local_sem):
        self.src, self.out, self.send, self.recv = src, out, send, recv
        self.major, self.minor, self.groups = split_index("expert", ranks)
        self.me = 2 * self.major + self.minor
        self.partner = 2 * self.major + 1 - self.minor
        self.copies = []
        self.keep = pltpu.make_async_copy(src, out.at[self.me], local_sem)

    def push(self, src, shard, slot, peer):
        copy = pltpu.make_async_remote_copy(
            src_ref=src, dst_ref=self.out.at[shard], send_sem=self.send.at[slot], recv_sem=self.recv.at[shard],
            device_id={"expert": peer}, device_id_type=MESH,
        )
        copy.start()
        self.copies.append(copy)

    def arrived(self, shard):
        pltpu.make_async_remote_copy(
            src_ref=self.out.at[shard], dst_ref=self.out.at[shard], send_sem=self.send.at[0],
            recv_sem=self.recv.at[shard], device_id={"expert": self.partner}, device_id_type=MESH,
        ).wait_recv()

    def start(self):
        self.keep.start()
        self.push(self.src, self.me, 0, self.partner)
        for k in range(1, self.groups):
            self.push(self.src, self.me, k, 2 * lax.rem(self.major + k, self.groups) + self.minor)

    def forward(self, k):
        shard = 2 * lax.rem(self.major - k + self.groups, self.groups) + self.minor
        self.arrived(shard)
        self.push(self.out.at[shard], shard, self.groups + k - 1, self.partner)

    def finish(self):
        for k in range(self.groups):
            self.arrived(2 * lax.rem(self.major - k + self.groups, self.groups) + 1 - self.minor)
        self.keep.wait()

    def drain(self):
        for copy in self.copies:
            copy.wait_send()


class Job:
    def __init__(self, axis, size, source, land, got, sems, window):
        self.axis, self.source, self.land, self.got, self.window = axis, source, land, got, window
        self.s1, self.r1, self.s2, self.r2 = sems
        self.major, self.minor, self.groups = split_index(axis, size)
        self.partner = 2 * self.major + 1 - self.minor
        self.copies = []
        self.unsent = list(range(1, self.groups)) + [0]
        self.unsummed = list(self.unsent)

    def remote(self, src, dst, s, r, peer):
        return pltpu.make_async_remote_copy(
            src_ref=src, dst_ref=dst, send_sem=s, recv_sem=r, device_id={self.axis: peer}, device_id_type=MESH
        )

    def target(self, k):
        return lax.rem(self.major + k, self.groups)

    def own(self, k):
        return self.source.at[2 * self.target(k) + self.minor]

    def send_next(self):
        if self.unsent:
            k = self.unsent.pop(0)
            copy = self.remote(
                self.source.at[2 * self.target(k) + 1 - self.minor], self.land.at[k], self.s1.at[k], self.r1.at[k],
                self.partner,
            )
            copy.start()
            self.copies.append(copy)

    def exchange(self):
        for _ in range(self.window):
            self.send_next()

    def sum_next(self):
        if not self.unsummed:
            return
        k = self.unsummed.pop(0)
        self.remote(self.land.at[k], self.land.at[k], self.s1.at[k], self.r1.at[k], self.partner).wait_recv()
        self.send_next()
        if k:
            own = self.own(k)
            own[...] = (own[...].astype(F32) + self.land[k].astype(F32)).astype(BF16)
            copy = self.remote(
                own, self.got.at[k - 1], self.s2.at[k - 1], self.r2.at[k - 1], 2 * self.target(k) + self.minor
            )
            copy.start()
            self.copies.append(copy)

    def finish(self):
        total = self.own(0)[...].astype(F32) + self.land[0].astype(F32)
        for k in range(1, self.groups):
            slot = self.got.at[k - 1]
            self.remote(slot, slot, self.s2.at[k - 1], self.r2.at[k - 1], self.partner).wait_recv()
            total = total + self.got[k - 1].astype(F32)
        return total.astype(BF16)

    def drain(self):
        for copy in self.copies:
            copy.wait_send()


def layer_kernel(ranks, groups_dp, exp_dev, cap, *refs):
    (ids_in, tok_in, cot_in, wg_in, wu_in, wd_in), refs = refs[:6], refs[6:]
    (out_o, out_t, out_g, out_u, out_d), refs = refs[:5], refs[5:]
    (ids_all, x_all, c_all, wg, wu, wd, pick, pick_w, x_rows, do_rows, eo), refs = refs[:11], refs[11:]
    (pre_g, pre_u, hid, gg, ug, wpart, land_e, got_e, land_w, got_w), refs = refs[:10], refs[10:]
    (g_send, g_recv, g_local, w_sem), refs = refs[:4], refs[4:]
    sems_e, sems_w = refs[:4], refs[4:]
    rows = tok_in.shape[0]
    span = wpart.shape[-1]
    groups = ranks // 2
    chunk = min(8, ranks) * cap
    parts = [slice(i, i + chunk) for i in range(0, ranks * cap, chunk)]

    loads = [pltpu.make_async_copy(a, b, w_sem.at[i]) for i, (a, b) in enumerate(((wg_in, wg), (wu_in, wu), (wd_in, wd)))]
    for load in loads:
        load.start()
    greet([("expert", ranks), ("dp", groups_dp)])
    g_ids, g_tok, g_cot = [
        Gather(ranks, src, out, g_send.at[t], g_recv.at[t], g_local.at[t])
        for t, (src, out) in enumerate(((ids_in, ids_all), (tok_in, x_all), (cot_in, c_all)))
    ]
    g_ids.start()
    g_tok.start()
    for k in range(1, groups):
        g_ids.forward(k)
    g_ids.finish()

    first = lax.axis_index("expert") * exp_dev
    sub = lax.broadcasted_iota(jnp.int32, (8, rows), 0)
    earlier = (
        lax.broadcasted_iota(jnp.int32, (rows, rows), 0) < lax.broadcasted_iota(jnp.int32, (rows, rows), 1)
    ).astype(F32).astype(BF16)
    slots = lax.broadcasted_iota(jnp.int32, (cap, rows), 0).astype(F32)

    def place(b, carry):
        packed = ids_all[b]
        named, num = packed >> 9, packed & 511
        match = jnp.zeros((8, rows), F32)
        weight = jnp.zeros((8, rows), F32)
        for k in range(packed.shape[0]):
            hit = named[k : k + 1, :] == first + sub
            match = match + jnp.where(hit, 1.0, 0.0)
            weight = weight + jnp.where(hit, num[k : k + 1, :].astype(F32), 0.0)
        weight = weight / DENOM
        rank = dot(match.astype(BF16), earlier, 1, 0)
        slot = jnp.where(match > 0.0, rank, -1.0)
        for e in range(exp_dev):
            here = slot[e : e + 1, :] == slots
            pick[b, e * cap : (e + 1) * cap, :] = jnp.where(here, 1.0, 0.0).astype(BF16)
            pick_w[b, e * cap : (e + 1) * cap, :] = jnp.where(here, weight[e : e + 1, :], 0.0).astype(BF16)
        return carry

    lax.fori_loop(0, ranks, place, 0)

    def to_slots(sel, vals, into):
        def one(b, carry):
            got = dot(sel[b], vals[b], 1, 0).astype(BF16)
            for e in range(exp_dev):
                into[e, pl.ds(pl.multiple_of(b * cap, cap), cap), :] = got[e * cap : (e + 1) * cap, :]
            return carry

        lax.fori_loop(0, ranks, one, 0)

    def from_slots(sel, vals, into):
        def one(b, carry):
            here = jnp.concatenate(
                [vals[e, pl.ds(pl.multiple_of(b * cap, cap), cap), :] for e in range(exp_dev)], axis=0
            )
            into[b] = dot(sel[b], here, 0, 0).astype(BF16)
            return carry

        lax.fori_loop(0, ranks, one, 0)

    for k in range(1, groups):
        g_tok.forward(k)
    g_cot.start()
    g_tok.finish()
    to_slots(pick, x_all, x_rows)
    for load in loads:
        load.wait()
    ahead = list(range(1, groups))
    for e in range(exp_dev):
        for part in parts:
            xr = x_rows[e, part, :]
            gate = dot(xr, wg[e], 1, 0)
            up = dot(xr, wu[e], 1, 0)
            pre_g[e, part, :] = gate
            pre_u[e, part, :] = up
            hid[e, part, :] = (gate * jax.nn.sigmoid(gate) * up).astype(BF16)
        if ahead:
            g_cot.forward(ahead.pop(0))
        for part in parts:
            eo[e, part, :] = dot(hid[e, part, :], wd[e], 1, 0).astype(BF16)
    for k in ahead:
        g_cot.forward(k)
    g_tok.drain()
    from_slots(pick_w, eo, x_all)
    job_o, job_t = [
        Job("expert", ranks, part, land_e.at[j], got_e.at[j], [s.at[j] for s in sems_e], 2)
        for j, part in enumerate((x_all, c_all))
    ]
    job_o.exchange()
    g_cot.finish()
    to_slots(pick_w, c_all, do_rows)

    w_jobs = []
    for e in range(exp_dev):
        mine = [
            Job("dp", groups_dp, wpart.at[j, e], land_w.at[j, e], got_w.at[j, e], [s.at[j, e] for s in sems_w], groups_dp)
            for j in range(3)
        ]
        for part in parts:
            gate, up = pre_g[e, part, :], pre_u[e, part, :]
            hidden_grad = dot(do_rows[e, part, :], wd[e], 1, 1)
            sig = jax.nn.sigmoid(gate)
            gg[part, :] = (hidden_grad * up * sig * (1.0 + gate * (1.0 - sig))).astype(BF16)
            ug[part, :] = (hidden_grad * (gate * sig)).astype(BF16)
        for j, (left, right) in ((2, (hid[e], do_rows)), (0, (gg[...], x_rows)), (1, (ug[...], x_rows))):
            for i in range(groups_dp):
                wpart[j, e, i] = dot(left, right[e, :, i * span : (i + 1) * span], 0, 0).astype(BF16)
            mine[j].exchange()
        for part in parts:
            eo[e, part, :] = (dot(gg[part, :], wg[e], 1, 1) + dot(ug[part, :], wu[e], 1, 1)).astype(BF16)
        job_o.sum_next()
        for job in w_jobs[3 * e - 3 :]:
            for _ in range(job.groups):
                job.sum_next()
        w_jobs += mine
    g_cot.drain()
    from_slots(pick, eo, c_all)
    job_t.exchange()
    for job in w_jobs[-3:]:
        for _ in range(job.groups):
            job.sum_next()
    for _ in range(groups):
        job_o.sum_next()
    for _ in range(groups):
        job_t.sum_next()
    out_o[...] = job_o.finish()
    out_t[...] = job_t.finish()
    for n, job in enumerate(w_jobs):
        (out_g, out_u, out_d)[n % 3][n // 3] = job.finish()
    for job in [g_ids, job_o, job_t] + w_jobs:
        job.drain()


def local(tokens, expert_ids, route_num, w_gate, w_up, w_down, cotangent):
    ranks, groups_dp = lax.axis_size("expert"), lax.axis_size("dp")
    exp_dev, width, ff = w_gate.shape
    rows = tokens.shape[0]
    capacity = 5 * rows // 16
    cap = -(-capacity // 16) * 16
    span = width // groups_dp
    m_e, m_d = ranks // 2, groups_dp // 2
    packed = (expert_ids * 512 + route_num).T

    def sems(lead, groups):
        return [pltpu.SemaphoreType.DMA((*lead, groups)) for _ in range(4)]

    grad_t = jax.ShapeDtypeStruct((exp_dev, ff, span), BF16)
    out, tgrad, gate_t, up_t, down = pl.pallas_call(
        functools.partial(layer_kernel, ranks, groups_dp, exp_dev, cap),
        out_shape=[jax.ShapeDtypeStruct((rows, width), BF16)] * 2 + [grad_t] * 3,
        in_specs=[ANY] * 6,
        out_specs=[VMEM] * 5,
        scratch_shapes=[
            pltpu.VMEM((ranks, *packed.shape), jnp.int32),
            pltpu.VMEM((ranks, rows, width), BF16),
            pltpu.VMEM((ranks, rows, width), BF16),
            pltpu.VMEM(w_gate.shape, BF16),
            pltpu.VMEM(w_up.shape, BF16),
            pltpu.VMEM(w_down.shape, BF16),
            pltpu.VMEM((ranks, exp_dev * cap, rows), BF16),
            pltpu.VMEM((ranks, exp_dev * cap, rows), BF16),
            pltpu.VMEM((exp_dev, ranks * cap, width), BF16),
            pltpu.VMEM((exp_dev, ranks * cap, width), BF16),
            pltpu.VMEM((exp_dev, ranks * cap, width), BF16),
            pltpu.VMEM((exp_dev, ranks * cap, ff), F32),
            pltpu.VMEM((exp_dev, ranks * cap, ff), F32),
            pltpu.VMEM((exp_dev, ranks * cap, ff), BF16),
            pltpu.VMEM((ranks * cap, ff), BF16),
            pltpu.VMEM((ranks * cap, ff), BF16),
            pltpu.VMEM((3, exp_dev, groups_dp, ff, span), BF16),
            pltpu.VMEM((2, m_e, rows, width), BF16),
            pltpu.VMEM((2, m_e - 1, rows, width), BF16),
            pltpu.VMEM((3, exp_dev, m_d, ff, span), BF16),
            pltpu.VMEM((3, exp_dev, m_d - 1, ff, span), BF16),
            pltpu.SemaphoreType.DMA((3, ranks)),
            pltpu.SemaphoreType.DMA((3, ranks)),
            pltpu.SemaphoreType.DMA((3,)),
            pltpu.SemaphoreType.DMA((3,)),
            *sems((2,), m_e),
            *sems((3, exp_dev), m_d),
        ],
        compiler_params=pltpu.CompilerParams(
            collective_id=0, has_side_effects=True, vmem_limit_bytes=60 * 1024 * 1024
        ),
    )(packed, tokens, cotangent, w_gate, w_up, w_down)
    return out, tgrad, gate_t.transpose(0, 2, 1), up_t.transpose(0, 2, 1), down


def solution(mesh):
    in_specs = (
        P(("dp", "expert"), None),
        P(("dp", "expert"), None),
        P(("dp", "expert"), None),
        P("expert", None, None),
        P("expert", None, None),
        P("expert", None, None),
        P(("dp", "expert"), None),
    )
    out_specs = (
        P(("dp", "expert"), None),
        P(("dp", "expert"), None),
        P("expert", "dp", None),
        P("expert", "dp", None),
        P("expert", None, "dp"),
    )
    return jax.shard_map(local, mesh=mesh, in_specs=in_specs, out_specs=out_specs, check_vma=False)
```

time: 395 us -> 138 us (0.35)
  waiting for transfers between devices: 299 us -> 0 us
  Pallas kernels: 0 us -> 127 us
  matrix products: 40 us -> 0 us
  blocking collectives: 32.4 us -> 0 us
  between operations: 14.3 us -> 0.67 us
    reduce_scatter x5 -> x0, waiting for transfers between devices: 233 us -> none  [the longest x2 111 us: from_slots(): lax.psum_scatter(part.reshape(ranks * rows, width), 'expert', scatter_dim...]
    pallas_call x0 -> x1, Pallas kernels: none -> 127 us  [local(): pl.pallas_call(functools.partial(layer_kernel, ranks, groups_dp, exp_dev,...]
    all_gather x2 -> x0, waiting for transfers between devices: 64.6 us -> none  [the longest x1 45.7 us: local(): x_all = lax.all_gather(tokens, 'expert')]
    dot_general x14 -> x0, matrix products: 40 us -> none  [the longest x1 5.85 us: local(): jnp.einsum('erd,erf->edf', x_rows, gate_grad, preferred_element_type=f32)]
    all_gather x1 -> x0, blocking collectives: 32.4 us -> none  [local(): packed = lax.all_gather(expert_ids * 512 + route_num, 'expert')]
  transfers between devices with their start and end apart: 7 -> 0, of which waited for: 7 -> 0; matrix products, arithmetic and copies ran while one was open for 8% -> 0% of each run, Pallas kernels for 0% -> 0%
where the time goes in v2:
time: 138 us; the launch traced here: 136 us
  Pallas kernels  127 us (92%)
  local copies, waits for them, and re-layouts  6.97 us (5%)
    pallas_call x1, Pallas kernels, local(): pl.pallas_call(functools.partial(layer_kernel, ranks, groups_dp, exp_dev,...  127 us
    unnamed x11, local copies, waits for them, and re-layouts  6.97 us

profile of v2, /device:TPU:0, one launch (start us, length us, event | category | flops | bytes accessed | tf_op | source)
XLA Modules:
  0.0 135.9 jit_solution(3322589022065600425)
XLA Ops:
  0.6 1.3 add_bitcast_fusion.refs_0_
  1.9 127.0 %shard_map.110 = (bf16[128,1024]{1,0:T(8,128)(2,1)}, bf16[128,1024]{1,0:T(8,128)(2,1)}, bf16[4,384,256]{2,1,0:T(8,128)(2,1)}, bf16[4,384,256]{2,1,0:T(8,128)(2,1)}, bf16[4,384,256]{2,1,0:T(8,128)(2,1)}) custom-call(s32[8,128]{1,0:T(8,128)} %add_bitcast_fusion.refs_0_, bf16[128,1024]{1,0:T(8,128)(2,1)} %refs_1_.1, bf16[128,1024]{1,0:T(8,128)(2,1)} %refs_2_.1, ...), custom_call_target="tpu_custom_call" | custom-call | tf_op jit(solution)/shard_map/pallas_call | solution.py:306
  128.9 0.0 copy-start.2
  128.9 0.0 copy-start.1
  128.9 0.0 copy-start
  129.0 2.4 %copy.12 = bf16[4,256,384]{2,1,0:T(8,128)(2,1)} copy(bf16[4,256,384]{1,2,0:T(8,128)(2,1)} %bitcast.5) | data formatting | bytes 1572864
  131.3 2.3 %copy.13 = bf16[4,256,384]{2,1,0:T(8,128)(2,1)} copy(bf16[4,256,384]{1,2,0:T(8,128)(2,1)} %bitcast.4) | data formatting | bytes 1572864
  133.6 0.0 copy-done.2
  133.6 0.7 copy.17
  134.3 0.0 copy-done.1
  134.3 0.7 copy.18
  135.0 0.0 copy-done
  135.0 0.9 copy.19
Async XLA Ops:
  128.9 4.7 %copy-start.2 = (bf16[128,1024]{1,0:T(8,128)(2,1)S(1)}, bf16[128,1024]{1,0:T(8,128)(2,1)}, u32[]{:S(2)}) copy-start(bf16[128,1024]{1,0:T(8,128)(2,1)} %get-tuple-element.25) | copy-start | bytes 786436
  128.9 5.4 %copy-start.1 = (bf16[128,1024]{1,0:T(8,128)(2,1)S(1)}, bf16[128,1024]{1,0:T(8,128)(2,1)}, u32[]{:S(2)}) copy-start(bf16[128,1024]{1,0:T(8,128)(2,1)} %get-tuple-element.26) | copy-start | bytes 786436
  128.9 6.1 %copy-start = (bf16[4,384,256]{2,1,0:T(8,128)(2,1)S(1)}, bf16[4,384,256]{2,1,0:T(8,128)(2,1)}, u32[]{:S(2)}) copy-start(bf16[4,384,256]{2,1,0:T(8,128)(2,1)} %get-tuple-element.29) | copy-start | bytes 2359300

commit v3 on v2

--- a/solution.py
+++ b/solution.py
@@ -32,62 +32,86 @@
     pl.semaphore_wait(barrier, count)
 
 
+def near_first(groups):
+    return sorted(range(1, groups), key=lambda k: min(k, groups - k))
+
+
 def dot(a, b, ca, cb):
     return lax.dot_general(a, b, (((ca,), (cb,)), ((), ())), preferred_element_type=F32)
 
 
 class Gather:
-    def __init__(self, ranks, src, out, send, recv, local_sem):
-        self.src, self.out, self.send, self.recv = src, out, send, recv
+    def __init__(self, ranks, src, out, part, send, recv, local_sem):
+        self.src, self.out, self.part, self.send, self.recv = src.at[part], out, part, send, recv
         self.major, self.minor, self.groups = split_index("expert", ranks)
         self.me = 2 * self.major + self.minor
         self.partner = 2 * self.major + 1 - self.minor
         self.copies = []
-        self.keep = pltpu.make_async_copy(src, out.at[self.me], local_sem)
+        self.keep = pltpu.make_async_copy(self.src, self.at(self.me), local_sem)
+
+    def at(self, shard):
+        return self.out.at[shard, self.part]
 
     def push(self, src, shard, slot, peer):
         copy = pltpu.make_async_remote_copy(
-            src_ref=src, dst_ref=self.out.at[shard], send_sem=self.send.at[slot], recv_sem=self.recv.at[shard],
+            src_ref=src, dst_ref=self.at(shard), send_sem=self.send.at[slot], recv_sem=self.recv.at[shard],
             device_id={"expert": peer}, device_id_type=MESH,
         )
         copy.start()
-        self.copies.append(copy)
+        return copy
 
     def arrived(self, shard):
         pltpu.make_async_remote_copy(
-            src_ref=self.out.at[shard], dst_ref=self.out.at[shard], send_sem=self.send.at[0],
+            src_ref=self.at(shard), dst_ref=self.at(shard), send_sem=self.send.at[0],
             recv_sem=self.recv.at[shard], device_id={"expert": self.partner}, device_id_type=MESH,
         ).wait_recv()
 
+    def to_peer(self, k):
+        self.peer_copy = self.push(self.src, self.me, k, 2 * lax.rem(self.major + k, self.groups) + self.minor)
+
     def start(self):
+        self.to_peer(near_first(self.groups)[0])
+        self.copies.append(self.push(self.src, self.me, 0, self.partner))
         self.keep.start()
-        self.push(self.src, self.me, 0, self.partner)
-        for k in range(1, self.groups):
-            self.push(self.src, self.me, k, 2 * lax.rem(self.major + k, self.groups) + self.minor)
+
+    def sent(self):
+        for copy in self.copies:
+            copy.wait_send()
+        self.copies = []
 
     def forward(self, k):
         shard = 2 * lax.rem(self.major - k + self.groups, self.groups) + self.minor
         self.arrived(shard)
-        self.push(self.out.at[shard], shard, self.groups + k - 1, self.partner)
+        self.copies.append(self.push(self.at(shard), shard, self.groups + k - 1, self.partner))
 
     def finish(self):
         for k in range(self.groups):
             self.arrived(2 * lax.rem(self.major - k + self.groups, self.groups) + 1 - self.minor)
         self.keep.wait()
 
-    def drain(self):
-        for copy in self.copies:
-            copy.wait_send()
+
+def gather_step(halves, i, following=()):
+    order = near_first(halves[0].groups)
+    last = i + 1 == len(order)
+    for g in halves:
+        g.peer_copy.wait_send()
+        if not last:
+            g.to_peer(order[i + 1])
+    for g in following if last else ():
+        g.start()
+    for g in halves:
+        g.forward(order[i])
 
 
 class Job:
-    def __init__(self, axis, size, source, land, got, sems, window):
+    def __init__(self, axis, size, source, land, got, sems, window, part=slice(None)):
+        self.part = part
         self.axis, self.source, self.land, self.got, self.window = axis, source, land, got, window
         self.s1, self.r1, self.s2, self.r2 = sems
         self.major, self.minor, self.groups = split_index(axis, size)
         self.partner = 2 * self.major + 1 - self.minor
         self.copies = []
-        self.unsent = list(range(1, self.groups)) + [0]
+        self.unsent = near_first(self.groups)[::-1] + [0]
         self.unsummed = list(self.unsent)
 
     def remote(self, src, dst, s, r, peer):
@@ -99,13 +123,13 @@
         return lax.rem(self.major + k, self.groups)
 
     def own(self, k):
-        return self.source.at[2 * self.target(k) + self.minor]
+        return self.source.at[2 * self.target(k) + self.minor, self.part]
 
     def send_next(self):
         if self.unsent:
             k = self.unsent.pop(0)
             copy = self.remote(
-                self.source.at[2 * self.target(k) + 1 - self.minor], self.land.at[k], self.s1.at[k], self.r1.at[k],
+                self.source.at[2 * self.target(k) + 1 - self.minor, self.part], self.land.at[k], self.s1.at[k], self.r1.at[k],
                 self.partner,
             )
             copy.start()
@@ -130,13 +154,17 @@
             copy.start()
             self.copies.append(copy)
 
+    def sum_ahead(self):
+        for _ in range(self.groups - 1):
+            self.sum_next()
+
     def finish(self):
         total = self.own(0)[...].astype(F32) + self.land[0].astype(F32)
         for k in range(1, self.groups):
             slot = self.got.at[k - 1]
             self.remote(slot, slot, self.s2.at[k - 1], self.r2.at[k - 1], self.partner).wait_recv()
             total = total + self.got[k - 1].astype(F32)
-        return total.astype(BF16)
+        return total
 
     def drain(self):
         for copy in self.copies:
@@ -160,15 +188,21 @@
     for load in loads:
         load.start()
     greet([("expert", ranks), ("dp", groups_dp)])
-    g_ids, g_tok, g_cot = [
-        Gather(ranks, src, out, g_send.at[t], g_recv.at[t], g_local.at[t])
-        for t, (src, out) in enumerate(((ids_in, ids_all), (tok_in, x_all), (cot_in, c_all)))
-    ]
-    g_ids.start()
-    g_tok.start()
-    for k in range(1, groups):
-        g_ids.forward(k)
-    g_ids.finish()
+    half = rows // 2
+    halves = (slice(0, half), slice(half, rows))
+
+    def gather(t, src, out, part):
+        return Gather(ranks, src, out, part, g_send.at[t], g_recv.at[t], g_local.at[t])
+
+    g_ids = [gather(0, ids_in, ids_all, slice(None))]
+    g_tok = [gather(1 + h, tok_in, x_all, halves[h]) for h in range(2)]
+    g_cot = [gather(3 + h, cot_in, c_all, halves[h]) for h in range(2)]
+    steps = range(groups - 1)
+    for g in g_ids + g_tok:
+        g.start()
+    for i in steps:
+        gather_step(g_ids, i)
+    g_ids[0].finish()
 
     first = lax.axis_index("expert") * exp_dev
     sub = lax.broadcasted_iota(jnp.int32, (8, rows), 0)
@@ -216,14 +250,14 @@
 
         lax.fori_loop(0, ranks, one, 0)
 
-    for k in range(1, groups):
-        g_tok.forward(k)
-    g_cot.start()
-    g_tok.finish()
+    for i in steps:
+        gather_step(g_tok, i, g_cot)
+    for g in g_tok:
+        g.finish()
     to_slots(pick, x_all, x_rows)
     for load in loads:
         load.wait()
-    ahead = list(range(1, groups))
+    ahead = list(steps)
     for e in range(exp_dev):
         for part in parts:
             xr = x_rows[e, part, :]
@@ -233,19 +267,25 @@
             pre_u[e, part, :] = up
             hid[e, part, :] = (gate * jax.nn.sigmoid(gate) * up).astype(BF16)
         if ahead:
-            g_cot.forward(ahead.pop(0))
+            gather_step(g_cot, ahead.pop(0))
         for part in parts:
             eo[e, part, :] = dot(hid[e, part, :], wd[e], 1, 0).astype(BF16)
-    for k in ahead:
-        g_cot.forward(k)
-    g_tok.drain()
+    for i in ahead:
+        gather_step(g_cot, i)
+    for g in g_tok:
+        g.sent()
     from_slots(pick_w, eo, x_all)
-    job_o, job_t = [
-        Job("expert", ranks, part, land_e.at[j], got_e.at[j], [s.at[j] for s in sems_e], 2)
-        for j, part in enumerate((x_all, c_all))
+    jobs_o, jobs_t = [
+        [
+            Job("expert", ranks, whole, land_e.at[j, h], got_e.at[j, h], [s.at[j, h] for s in sems_e], 1, halves[h])
+            for h in range(2)
+        ]
+        for j, whole in enumerate((x_all, c_all))
     ]
-    job_o.exchange()
-    g_cot.finish()
+    for job in jobs_o:
+        job.exchange()
+    for g in g_cot:
+        g.finish()
     to_slots(pick_w, c_all, do_rows)
 
     w_jobs = []
@@ -254,39 +294,60 @@
             Job("dp", groups_dp, wpart.at[j, e], land_w.at[j, e], got_w.at[j, e], [s.at[j, e] for s in sems_w], groups_dp)
             for j in range(3)
         ]
+        def weight_part(j, left, right):
+            for i in range(groups_dp):
+                wpart[j, e, i] = dot(left, right[e, :, i * span : (i + 1) * span], 0, 0).astype(BF16)
+            mine[j].exchange()
+
+        weight_part(2, hid[e], do_rows)
         for part in parts:
             gate, up = pre_g[e, part, :], pre_u[e, part, :]
             hidden_grad = dot(do_rows[e, part, :], wd[e], 1, 1)
             sig = jax.nn.sigmoid(gate)
             gg[part, :] = (hidden_grad * up * sig * (1.0 + gate * (1.0 - sig))).astype(BF16)
             ug[part, :] = (hidden_grad * (gate * sig)).astype(BF16)
-        for j, (left, right) in ((2, (hid[e], do_rows)), (0, (gg[...], x_rows)), (1, (ug[...], x_rows))):
-            for i in range(groups_dp):
-                wpart[j, e, i] = dot(left, right[e, :, i * span : (i + 1) * span], 0, 0).astype(BF16)
-            mine[j].exchange()
+        mine[2].sum_ahead()
+        weight_part(0, gg[...], x_rows)
+        weight_part(1, ug[...], x_rows)
+        mine[0].sum_ahead()
         for part in parts:
             eo[e, part, :] = (dot(gg[part, :], wg[e], 1, 1) + dot(ug[part, :], wu[e], 1, 1)).astype(BF16)
-        job_o.sum_next()
-        for job in w_jobs[3 * e - 3 :]:
-            for _ in range(job.groups):
+        mine[1].sum_ahead()
+        for job in jobs_o:
+            job.sum_next()
+        w_jobs += mine
+    for g in g_cot:
+        g.sent()
+    from_slots(pick, eo, c_all)
+    for job in jobs_t:
+        job.exchange()
+    for jobs in (jobs_o, jobs_t):
+        for _ in range(groups):
+            for job in jobs:
                 job.sum_next()
-        w_jobs += mine
-    g_cot.drain()
-    from_slots(pick, eo, c_all)
-    job_t.exchange()
-    for job in w_jobs[-3:]:
-        for _ in range(job.groups):
-            job.sum_next()
-    for _ in range(groups):
-        job_o.sum_next()
-    for _ in range(groups):
-        job_t.sum_next()
-    out_o[...] = job_o.finish()
-    out_t[...] = job_t.finish()
+    for job in w_jobs:
+        job.sum_next()
     for n, job in enumerate(w_jobs):
-        (out_g, out_u, out_d)[n % 3][n // 3] = job.finish()
-    for job in [g_ids, job_o, job_t] + w_jobs:
+        total = job.finish()
+        if n % 3 == 2:
+            out_d[n // 3] = total.astype(BF16)
+        else:
+            (out_g, out_u)[n % 3][n // 3] = total.T.astype(BF16)
+    for jobs, out in ((jobs_o, out_o), (jobs_t, out_t)):
+        for job in jobs:
+            out[job.part, :] = job.finish().astype(BF16)
+    for job in jobs_o + jobs_t + w_jobs:
         job.drain()
+    for g in g_ids:
+        g.sent()
+
+
+def copy_kernel(*refs):
+    copies = [pltpu.make_async_copy(a, b, refs[10].at[i]) for i, (a, b) in enumerate(zip(refs[:5], refs[5:10]))]
+    for copy in copies:
+        copy.start()
+    for copy in copies:
+        copy.wait()
 
 
 def local(tokens, expert_ids, route_num, w_gate, w_up, w_down, cotangent):
@@ -302,10 +363,12 @@
     def sems(lead, groups):
         return [pltpu.SemaphoreType.DMA((*lead, groups)) for _ in range(4)]
 
-    grad_t = jax.ShapeDtypeStruct((exp_dev, ff, span), BF16)
-    out, tgrad, gate_t, up_t, down = pl.pallas_call(
+    grad = jax.ShapeDtypeStruct((exp_dev, span, ff), BF16)
+    out_shape = [jax.ShapeDtypeStruct((rows, width), BF16)] * 2 + [grad] * 2
+    out_shape += [jax.ShapeDtypeStruct((exp_dev, ff, span), BF16)]
+    results = pl.pallas_call(
         functools.partial(layer_kernel, ranks, groups_dp, exp_dev, cap),
-        out_shape=[jax.ShapeDtypeStruct((rows, width), BF16)] * 2 + [grad_t] * 3,
+        out_shape=out_shape,
         in_specs=[ANY] * 6,
         out_specs=[VMEM] * 5,
         scratch_shapes=[
@@ -326,22 +389,25 @@
             pltpu.VMEM((ranks * cap, ff), BF16),
             pltpu.VMEM((ranks * cap, ff), BF16),
             pltpu.VMEM((3, exp_dev, groups_dp, ff, span), BF16),
-            pltpu.VMEM((2, m_e, rows, width), BF16),
-            pltpu.VMEM((2, m_e - 1, rows, width), BF16),
+            pltpu.VMEM((2, 2, m_e, rows // 2, width), BF16),
+            pltpu.VMEM((2, 2, m_e - 1, rows // 2, width), BF16),
             pltpu.VMEM((3, exp_dev, m_d, ff, span), BF16),
             pltpu.VMEM((3, exp_dev, m_d - 1, ff, span), BF16),
-            pltpu.SemaphoreType.DMA((3, ranks)),
-            pltpu.SemaphoreType.DMA((3, ranks)),
+            pltpu.SemaphoreType.DMA((5, ranks)),
+            pltpu.SemaphoreType.DMA((5, ranks)),
+            pltpu.SemaphoreType.DMA((5,)),
             pltpu.SemaphoreType.DMA((3,)),
-            pltpu.SemaphoreType.DMA((3,)),
-            *sems((2,), m_e),
+            *sems((2, 2), m_e),
             *sems((3, exp_dev), m_d),
         ],
         compiler_params=pltpu.CompilerParams(
             collective_id=0, has_side_effects=True, vmem_limit_bytes=60 * 1024 * 1024
         ),
     )(packed, tokens, cotangent, w_gate, w_up, w_down)
-    return out, tgrad, gate_t.transpose(0, 2, 1), up_t.transpose(0, 2, 1), down
+    return tuple(pl.pallas_call(
+        copy_kernel, out_shape=out_shape, in_specs=[ANY] * 5, out_specs=[ANY] * 5,
+        scratch_shapes=[pltpu.SemaphoreType.DMA((5,))],
+    )(*results))
 
 
 def solution(mesh):

time: 138 us -> 226 us (1.64)
  Pallas kernels: 127 us -> 222 us
  local copies, waits for them, and re-layouts: 6.97 us -> 0 us
    pallas_call x0 -> x1, Pallas kernels: none -> 88.5 us  [local(): pl.pallas_call(copy_kernel, out_shape=out_shape, in_specs=[ANY] * 5, out_...]
    unnamed x11 -> x0, local copies, waits for them, and re-layouts: 6.97 us -> none
    pallas_call x1, Pallas kernels: 127 us -> 134 us  [local(): pl.pallas_call(functools.partial(layer_kernel, ranks, groups_dp, exp_dev,...]
where the time goes in v3:
time: 226 us; the launch traced here: 224 us
  Pallas kernels  222 us (98%)
    pallas_call x1, Pallas kernels, local(): pl.pallas_call(functools.partial(layer_kernel, ranks, groups_dp, exp_dev,...  134 us
    pallas_call x1, Pallas kernels, local(): pl.pallas_call(copy_kernel, out_shape=out_shape, in_specs=[ANY] * 5, out_...  88.5 us

profile of v3, /device:TPU:0, one launch (start us, length us, event | category | flops | bytes accessed | tf_op | source)
XLA Modules:
  0.0 224.1 jit_solution(15340657362190935450)
XLA Ops:
  0.6 1.3 add_bitcast_fusion.refs_0_
  1.9 133.5 %shard_map.110 = (bf16[128,1024]{1,0:T(8,128)(2,1)}, bf16[128,1024]{1,0:T(8,128)(2,1)}, bf16[4,256,384]{2,1,0:T(8,128)(2,1)}, bf16[4,256,384]{2,1,0:T(8,128)(2,1)}, bf16[4,384,256]{2,1,0:T(8,128)(2,1)}) custom-call(s32[8,128]{1,0:T(8,128)} %add_bitcast_fusion.refs_0_, bf16[128,1024]{1,0:T(8,128)(2,1)} %refs_1_.1, bf16[128,1024]{1,0:T(8,128)(2,1)} %refs_2_.1, ...), custom_call_target="tpu_custom_call" | custom-call | tf_op jit(solution)/shard_map/pallas_call | solution.py:369
  135.5 88.5 %shard_map.111 = (bf16[128,1024]{1,0:T(8,128)(2,1)}, bf16[128,1024]{1,0:T(8,128)(2,1)}, bf16[4,256,384]{2,1,0:T(8,128)(2,1)}, bf16[4,256,384]{2,1,0:T(8,128)(2,1)}, bf16[4,384,256]{2,1,0:T(8,128)(2,1)}) custom-call(bf16[128,1024]{1,0:T(8,128)(2,1)} %get-tuple-element.10.refs_0_, bf16[128,1024]{1,0:T(8,128)(2,1)} %get-tuple-element.11.refs_1_, ...), custom_call_target="tpu_custom_call" | custom-call | tf_op jit(solution)/shard_map/pallas_call | solution.py:407

commit v4 on v3

--- a/solution.py
+++ b/solution.py
@@ -50,7 +50,7 @@
         self.keep = pltpu.make_async_copy(self.src, self.at(self.me), local_sem)
 
     def at(self, shard):
-        return self.out.at[shard, self.part]
+        return self.out.at[(shard, *self.part)]
 
     def push(self, src, shard, slot, peer):
         copy = pltpu.make_async_remote_copy(
@@ -66,13 +66,12 @@
             recv_sem=self.recv.at[shard], device_id={"expert": self.partner}, device_id_type=MESH,
         ).wait_recv()
 
-    def to_peer(self, k):
-        self.peer_copy = self.push(self.src, self.me, k, 2 * lax.rem(self.major + k, self.groups) + self.minor)
-
     def start(self):
-        self.to_peer(near_first(self.groups)[0])
+        self.keep.start()
         self.copies.append(self.push(self.src, self.me, 0, self.partner))
-        self.keep.start()
+        for k in near_first(self.groups):
+            peer = 2 * lax.rem(self.major + k, self.groups) + self.minor
+            self.copies.append(self.push(self.src, self.me, k, peer))
 
     def sent(self):
         for copy in self.copies:
@@ -88,19 +87,6 @@
         for k in range(self.groups):
             self.arrived(2 * lax.rem(self.major - k + self.groups, self.groups) + 1 - self.minor)
         self.keep.wait()
-
-
-def gather_step(halves, i, following=()):
-    order = near_first(halves[0].groups)
-    last = i + 1 == len(order)
-    for g in halves:
-        g.peer_copy.wait_send()
-        if not last:
-            g.to_peer(order[i + 1])
-    for g in following if last else ():
-        g.start()
-    for g in halves:
-        g.forward(order[i])
 
 
 class Job:
@@ -144,7 +130,8 @@
             return
         k = self.unsummed.pop(0)
         self.remote(self.land.at[k], self.land.at[k], self.s1.at[k], self.r1.at[k], self.partner).wait_recv()
-        self.send_next()
+        if self.axis == "expert":
+            self.send_next()
         if k:
             own = self.own(k)
             own[...] = (own[...].astype(F32) + self.land[k].astype(F32)).astype(BF16)
@@ -194,15 +181,20 @@
     def gather(t, src, out, part):
         return Gather(ranks, src, out, part, g_send.at[t], g_recv.at[t], g_local.at[t])
 
-    g_ids = [gather(0, ids_in, ids_all, slice(None))]
-    g_tok = [gather(1 + h, tok_in, x_all, halves[h]) for h in range(2)]
-    g_cot = [gather(3 + h, cot_in, c_all, halves[h]) for h in range(2)]
-    steps = range(groups - 1)
-    for g in g_ids + g_tok:
+    dp_major, _, dp_groups = split_index("dp", groups_dp)
+    wide = tok_in.shape[1] // 2
+    later = dp_major // (dp_groups // 2)
+    col_halves = [pl.ds(pl.multiple_of(c * wide, wide), wide) for c in (1 - later, later)]
+    every = slice(None)
+    g_ids = gather(0, ids_in, ids_all, (every, every))
+    g_tok = [gather(1 + h, tok_in, x_all, (halves[h], every)) for h in range(2)]
+    g_cot = [gather(3 + h, cot_in, c_all, (every, col_halves[h])) for h in range(2)]
+    order = near_first(groups)
+    for g in [g_ids] + g_tok:
         g.start()
-    for i in steps:
-        gather_step(g_ids, i)
-    g_ids[0].finish()
+    for k in order:
+        g_ids.forward(k)
+    g_ids.finish()
 
     first = lax.axis_index("expert") * exp_dev
     sub = lax.broadcasted_iota(jnp.int32, (8, rows), 0)
@@ -231,11 +223,11 @@
 
     lax.fori_loop(0, ranks, place, 0)
 
-    def to_slots(sel, vals, into):
+    def to_slots(sel, vals, into, cols):
         def one(b, carry):
-            got = dot(sel[b], vals[b], 1, 0).astype(BF16)
+            got = dot(sel[b], vals[b, :, cols], 1, 0).astype(BF16)
             for e in range(exp_dev):
-                into[e, pl.ds(pl.multiple_of(b * cap, cap), cap), :] = got[e * cap : (e + 1) * cap, :]
+                into[e, pl.ds(pl.multiple_of(b * cap, cap), cap), cols] = got[e * cap : (e + 1) * cap, :]
             return carry
 
         lax.fori_loop(0, ranks, one, 0)
@@ -250,14 +242,22 @@
 
         lax.fori_loop(0, ranks, one, 0)
 
-    for i in steps:
-        gather_step(g_tok, i, g_cot)
+    for g, following in zip(g_tok, g_cot):
+        for k in order:
+            g.forward(k)
+        following.start()
     for g in g_tok:
         g.finish()
-    to_slots(pick, x_all, x_rows)
+    to_slots(pick, x_all, x_rows, every)
     for load in loads:
         load.wait()
-    ahead = list(steps)
+    ahead = [(g, k) for g in g_cot for k in order]
+
+    def forward_next():
+        if ahead:
+            g, k = ahead.pop(0)
+            g.forward(k)
+
     for e in range(exp_dev):
         for part in parts:
             xr = x_rows[e, part, :]
@@ -266,15 +266,14 @@
             pre_g[e, part, :] = gate
             pre_u[e, part, :] = up
             hid[e, part, :] = (gate * jax.nn.sigmoid(gate) * up).astype(BF16)
-        if ahead:
-            gather_step(g_cot, ahead.pop(0))
+        forward_next()
         for part in parts:
             eo[e, part, :] = dot(hid[e, part, :], wd[e], 1, 0).astype(BF16)
-    for i in ahead:
-        gather_step(g_cot, i)
+        forward_next()
+    while ahead:
+        forward_next()
     for g in g_tok:
         g.sent()
-    from_slots(pick_w, eo, x_all)
     jobs_o, jobs_t = [
         [
             Job("expert", ranks, whole, land_e.at[j, h], got_e.at[j, h], [s.at[j, h] for s in sems_e], 1, halves[h])
@@ -282,31 +281,53 @@
         ]
         for j, whole in enumerate((x_all, c_all))
     ]
+    w_jobs = [
+        Job("dp", groups_dp, wpart.at[j, e], land_w.at[j, e], got_w.at[j, e], [s.at[j, e] for s in sems_w], window)
+        for e in range(exp_dev)
+        for j, window in ((0, groups_dp), (1, groups_dp), (2, dp_groups - 1))
+    ]
+
+    def weight_block(j, e, left, right, i):
+        cols = pl.ds(pl.multiple_of(i * span, span), span)
+        wpart[j, e, i] = dot(left, right[e, :, cols], 0, 0).astype(BF16)
+
+    def down_half(h):
+        g_cot[h].finish()
+        to_slots(pick_w, c_all, do_rows, col_halves[h])
+        for e in range(exp_dev):
+            for n in range(dp_groups):
+                weight_block(2, e, hid[e], do_rows, (later if h else 1 - later) * dp_groups + n)
+            if h == 0 and dp_groups == 2:
+                w_jobs[3 * e + 2].exchange()
+
+    down_half(0)
+    from_slots(pick_w, eo, x_all)
     for job in jobs_o:
         job.exchange()
-    for g in g_cot:
-        g.finish()
-    to_slots(pick_w, c_all, do_rows)
-
-    w_jobs = []
+    if dp_groups == 2:
+        for e in range(exp_dev):
+            w_jobs[3 * e + 2].sum_ahead()
+    down_half(1)
     for e in range(exp_dev):
-        mine = [
-            Job("dp", groups_dp, wpart.at[j, e], land_w.at[j, e], got_w.at[j, e], [s.at[j, e] for s in sems_w], groups_dp)
-            for j in range(3)
-        ]
+        if dp_groups != 2:
+            w_jobs[3 * e + 2].exchange()
+        w_jobs[3 * e + 2].send_next()
+    for e in range(exp_dev):
+        mine = w_jobs[3 * e : 3 * e + 3]
+
         def weight_part(j, left, right):
             for i in range(groups_dp):
-                wpart[j, e, i] = dot(left, right[e, :, i * span : (i + 1) * span], 0, 0).astype(BF16)
+                weight_block(j, e, left, right, i)
             mine[j].exchange()
 
-        weight_part(2, hid[e], do_rows)
         for part in parts:
             gate, up = pre_g[e, part, :], pre_u[e, part, :]
             hidden_grad = dot(do_rows[e, part, :], wd[e], 1, 1)
             sig = jax.nn.sigmoid(gate)
             gg[part, :] = (hidden_grad * up * sig * (1.0 + gate * (1.0 - sig))).astype(BF16)
             ug[part, :] = (hidden_grad * (gate * sig)).astype(BF16)
-        mine[2].sum_ahead()
+        if dp_groups != 2:
+            mine[2].sum_ahead()
         weight_part(0, gg[...], x_rows)
         weight_part(1, ug[...], x_rows)
         mine[0].sum_ahead()
@@ -315,7 +336,6 @@
         mine[1].sum_ahead()
         for job in jobs_o:
             job.sum_next()
-        w_jobs += mine
     for g in g_cot:
         g.sent()
     from_slots(pick, eo, c_all)
@@ -338,16 +358,12 @@
             out[job.part, :] = job.finish().astype(BF16)
     for job in jobs_o + jobs_t + w_jobs:
         job.drain()
-    for g in g_ids:
-        g.sent()
+    g_ids.sent()
 
 
 def copy_kernel(*refs):
-    copies = [pltpu.make_async_copy(a, b, refs[10].at[i]) for i, (a, b) in enumerate(zip(refs[:5], refs[5:10]))]
-    for copy in copies:
-        copy.start()
-    for copy in copies:
-        copy.wait()
+    for a, b in zip(refs[:5], refs[5:]):
+        b[...] = a[...]
 
 
 def local(tokens, expert_ids, route_num, w_gate, w_up, w_down, cotangent):
@@ -405,8 +421,8 @@
         ),
     )(packed, tokens, cotangent, w_gate, w_up, w_down)
     return tuple(pl.pallas_call(
-        copy_kernel, out_shape=out_shape, in_specs=[ANY] * 5, out_specs=[ANY] * 5,
-        scratch_shapes=[pltpu.SemaphoreType.DMA((5,))],
+        copy_kernel, out_shape=out_shape, in_specs=[VMEM] * 5, out_specs=[VMEM] * 5,
+        compiler_params=pltpu.CompilerParams(vmem_limit_bytes=16 * 1024 * 1024),
     )(*results))
 
 

time: 226 us -> 127 us (0.56)
  Pallas kernels: 222 us -> 119 us
  local copies, waits for them, and re-layouts: 0 us -> 5.29 us
    pallas_call x1, Pallas kernels: 88.5 us -> 1.79 us  [local(): pl.pallas_call(copy_kernel, out_shape=out_shape, in_specs=[VMEM] * 5, out...]
    pallas_call x1, Pallas kernels: 134 us -> 118 us  [local(): pl.pallas_call(functools.partial(layer_kernel, ranks, groups_dp, exp_dev,...]
    unnamed x0 -> x10, local copies, waits for them, and re-layouts: none -> 5.29 us
where the time goes in v4:
time: 127 us
  Pallas kernels  119 us (94%)
  local copies, waits for them, and re-layouts  5.29 us (4%)
  other arithmetic  1.3 us (1%)
    pallas_call x1, Pallas kernels, local(): pl.pallas_call(functools.partial(layer_kernel, ranks, groups_dp, exp_dev,...  118 us
    unnamed x10, local copies, waits for them, and re-layouts  5.29 us

profile of v4, /device:TPU:0, one launch (start us, length us, event | category | flops | bytes accessed | tf_op | source)
XLA Modules:
  0.0 126.7 jit_solution(15132933121177784207)
XLA Ops:
  0.6 1.3 %add_bitcast_fusion.refs_0_ = s32[8,128]{1,0:T(8,128)} fusion(s32[128,8]{0,1:T(8,128)} %param.9, s32[128,8]{0,1:T(8,128)} %param.8), kind=kLoop, calls=%fused_computation | loop fusion | flops 2048 | bytes 12288 | tf_op jit(solution)/shard_map/transpose | solution.py:377
  1.9 117.6 %shard_map.110 = (bf16[128,1024]{1,0:T(8,128)(2,1)}, bf16[128,1024]{1,0:T(8,128)(2,1)}, bf16[4,256,384]{2,1,0:T(8,128)(2,1)}, bf16[4,256,384]{2,1,0:T(8,128)(2,1)}, bf16[4,384,256]{2,1,0:T(8,128)(2,1)}) custom-call(s32[8,128]{1,0:T(8,128)} %add_bitcast_fusion.refs_0_, bf16[128,1024]{1,0:T(8,128)(2,1)} %refs_1_.1, bf16[128,1024]{1,0:T(8,128)(2,1)} %refs_2_.1, ...), custom_call_target="tpu_custom_call" | custom-call | tf_op jit(solution)/shard_map/pallas_call | solution.py:385
  119.6 0.0 copy-start
  119.6 1.1 copy-done
  120.7 0.0 copy-start.1
  120.7 1.1 copy-done.1
  121.8 0.0 copy-start.2
  121.8 1.1 copy-done.2
  123.0 0.0 copy-start.3
  123.0 0.9 copy-done.3
  123.9 0.0 copy-start.4
  123.9 0.9 copy-done.4
  124.9 1.8 %shard_map.111 = (bf16[128,1024]{1,0:T(8,128)(2,1)}, bf16[128,1024]{1,0:T(8,128)(2,1)}, bf16[4,256,384]{2,1,0:T(8,128)(2,1)}, bf16[4,256,384]{2,1,0:T(8,128)(2,1)}, bf16[4,384,256]{2,1,0:T(8,128)(2,1)}) custom-call(bf16[128,1024]{1,0:T(8,128)(2,1)S(1)} %copy-done.3, bf16[128,1024]{1,0:T(8,128)(2,1)S(1)} %copy-done.4, bf16[4,256,384]{2,1,0:T(8,128)(2,1)S(1)} %copy-done, ...), custom_call_target="tpu_custom_call" | custom-call | tf_op jit(solution)/shard_map/pallas_call | solution.py:423
Async XLA Ops:
  119.6 1.1 copy-start
  120.7 1.1 copy-start.1
  121.8 1.1 copy-start.2
  123.0 0.9 copy-start.3
  123.9 0.9 copy-start.4

commit v5 on v4

--- a/solution.py
+++ b/solution.py
@@ -362,8 +362,11 @@
 
 
 def copy_kernel(*refs):
-    for a, b in zip(refs[:5], refs[5:]):
-        b[...] = a[...]
+    copies = [pltpu.make_async_copy(a, b, refs[10].at[i]) for i, (a, b) in enumerate(zip(refs[:5], refs[5:10]))]
+    for copy in copies:
+        copy.start()
+    for copy in copies:
+        copy.wait()
 
 
 def local(tokens, expert_ids, route_num, w_gate, w_up, w_down, cotangent):
@@ -421,8 +424,9 @@
         ),
     )(packed, tokens, cotangent, w_gate, w_up, w_down)
     return tuple(pl.pallas_call(
-        copy_kernel, out_shape=out_shape, in_specs=[VMEM] * 5, out_specs=[VMEM] * 5,
-        compiler_params=pltpu.CompilerParams(vmem_limit_bytes=16 * 1024 * 1024),
+        copy_kernel, out_shape=out_shape, in_specs=[ANY] * 5, out_specs=[VMEM] * 5,
+        scratch_shapes=[pltpu.SemaphoreType.DMA((5,))],
+        compiler_params=pltpu.CompilerParams(vmem_limit_bytes=60 * 1024 * 1024),
     )(*results))
 
 

time: 127 us -> 123 us (0.969)
  local copies, waits for them, and re-layouts: 5.29 us -> 0 us
  Pallas kernels: 119 us -> 121 us
    unnamed x10 -> x0, local copies, waits for them, and re-layouts: 5.29 us -> none
    pallas_call x1, Pallas kernels: 1.79 us -> 3.39 us  [local(): pl.pallas_call(copy_kernel, out_shape=out_shape, in_specs=[ANY] * 5, out_...]
where the time goes in v5:
time: 123 us
  Pallas kernels  121 us (98%)
  other arithmetic  1.3 us (1%)
    pallas_call x1, Pallas kernels, local(): pl.pallas_call(functools.partial(layer_kernel, ranks, groups_dp, exp_dev,...  118 us
    pallas_call x1, Pallas kernels, local(): pl.pallas_call(copy_kernel, out_shape=out_shape, in_specs=[ANY] * 5, out_...  3.39 us

profile of v5, /device:TPU:0, one launch (start us, length us, event | category | flops | bytes accessed | tf_op | source)
XLA Modules:
  0.0 123.1 jit_solution(6481398162105456840)
XLA Ops:
  0.6 1.3 %add_bitcast_fusion.refs_0_ = s32[8,128]{1,0:T(8,128)} fusion(s32[128,8]{0,1:T(8,128)} %param.9, s32[128,8]{0,1:T(8,128)} %param.8), kind=kLoop, calls=%fused_computation | loop fusion | flops 2048 | bytes 12288 | tf_op jit(solution)/shard_map/transpose | solution.py:380
  1.9 117.6 %shard_map.110 = (bf16[128,1024]{1,0:T(8,128)(2,1)}, bf16[128,1024]{1,0:T(8,128)(2,1)}, bf16[4,256,384]{2,1,0:T(8,128)(2,1)}, bf16[4,256,384]{2,1,0:T(8,128)(2,1)}, bf16[4,384,256]{2,1,0:T(8,128)(2,1)}) custom-call(s32[8,128]{1,0:T(8,128)} %add_bitcast_fusion.refs_0_, bf16[128,1024]{1,0:T(8,128)(2,1)} %refs_1_.1, bf16[128,1024]{1,0:T(8,128)(2,1)} %refs_2_.1, ...), custom_call_target="tpu_custom_call" | custom-call | tf_op jit(solution)/shard_map/pallas_call | solution.py:388
  119.6 3.4 %shard_map.111 = (bf16[128,1024]{1,0:T(8,128)(2,1)}, bf16[128,1024]{1,0:T(8,128)(2,1)}, bf16[4,256,384]{2,1,0:T(8,128)(2,1)}, bf16[4,256,384]{2,1,0:T(8,128)(2,1)}, bf16[4,384,256]{2,1,0:T(8,128)(2,1)}) custom-call(bf16[128,1024]{1,0:T(8,128)(2,1)} %get-tuple-element.10.refs_0_, bf16[128,1024]{1,0:T(8,128)(2,1)} %get-tuple-element.11.refs_1_, ...), custom_call_target="tpu_custom_call" | custom-call | tf_op jit(solution)/shard_map/pallas_call | solution.py:426
